TPU v7x, 32 devices: a whole 2x2x4 slice. The times are simulated.
32 devices in a mesh: row: 8 (over y, x, core), col: 4 (over z).
Axes of the slice: x: 2, y: 2, z: 4, core: 2. Of those that a mesh axis runs over, the one named last changes fastest.
Arguments:
- features: bfloat16 [16384, 1024], P(('row', 'col')), may hold values from 0 to 4, as said below
- coords: float32 [64, 16384], P(None, ('row', 'col')), may hold values from -1 to 1
Outputs:
- placed: float32 [64, 16384], P(None, ('row', 'col'))
- row_stress: float32 [16384], P(('row', 'col'))
- stress_norm: float32 [], replicated
Inputs may be any that keep to these rules, and one draw needn't show every extreme that they name: `features`: every molecule has at least one nonzero feature.
All inputs are finite; a program needn't handle non-finite values.
Results may differ from a plain program's by a relative error of at most 0.0003.
Values may be sent and summed in bfloat16 or wider, within the bound.
A program may use at most 192 MiB of HBM per device.

v0:
```python
import jax
import jax.numpy as jnp
from jax import lax
from jax.sharding import PartitionSpec as P

ITERS = 2
FLOOR = 0.25
EXACT = lax.Precision.HIGHEST


def from_root(block, axis, owner):
    block = jnp.where(lax.axis_index(axis) == owner, block, jnp.zeros_like(block))
    return lax.psum(block, axis)


def squares_of(values):
    return jnp.einsum("rf,rf->r", values, values, preferred_element_type=jnp.float32)


def tanimoto(left_rows, left_sq, right_rows):
    right_sq = squares_of(right_rows)
    common = lax.dot_general(
        left_rows, right_rows, (((1,), (1,)), ((), ())), preferred_element_type=jnp.float32
    )
    return 1.0 - common / (left_sq[:, None] + right_sq[None, :] - common)


def guttman_terms(dissim, x_rows, x_cols):
    coord_dim, row_len = x_rows.shape
    block_len = min(512, row_len)
    block_count = row_len // block_len
    col_norms = jnp.sum(x_cols * x_cols, axis=0)
    dis_blocks = dissim.reshape(block_count, block_len, dissim.shape[1])
    x_blocks = jnp.moveaxis(x_rows.reshape(coord_dim, block_count, block_len), 1, 0)

    def one_block(inputs):
        dis_blk, x_blk = inputs
        blk_norms = jnp.sum(x_blk * x_blk, axis=0)
        inner = lax.dot_general(
            x_blk,
            x_cols,
            (((0,), (0,)), ((), ())),
            precision=EXACT,
            preferred_element_type=jnp.float32,
        )
        distance = jnp.sqrt(
            jnp.maximum(blk_norms[:, None] + col_norms[None, :] - 2.0 * inner, FLOOR * FLOOR)
        )
        ratios = dis_blk / distance
        pulled = lax.dot_general(
            x_cols,
            ratios,
            (((1,), (1,)), ((), ())),
            precision=EXACT,
            preferred_element_type=jnp.float32,
        )
        pull_terms = x_blk * jnp.sum(ratios, axis=1)[None, :] - pulled
        stress = jnp.sum(jnp.square(dis_blk - distance), axis=1)
        return (pull_terms, stress)

    pull_terms, stress = lax.map(one_block, (dis_blocks, x_blocks))
    return (jnp.moveaxis(pull_terms, 0, 1).reshape(coord_dim, row_len), stress.reshape(row_len))


def on_device(features, coords):
    rows_n = lax.axis_size("row")
    cols_n = lax.axis_size("col")
    row_at = lax.axis_index("row")
    col_at = lax.axis_index("col")
    ratio_k = rows_n // cols_n
    share_len = coords.shape[1]
    row_len = share_len * cols_n
    molecules = row_len * rows_n
    feature_rows = lax.all_gather(features, "col", axis=0, tiled=True)
    rows_sq = squares_of(feature_rows)
    pieces = []
    for offset in range(ratio_k):
        feature_cols = from_root(feature_rows, "row", col_at * ratio_k + offset)
        pieces.append(tanimoto(feature_rows, rows_sq, feature_cols))
    dissim = jnp.concatenate(pieces, axis=1)
    dissim_sq = jnp.sum(dissim * dissim)
    current = coords
    row_stress = jnp.zeros((share_len,), jnp.float32)
    for sweep in range(ITERS):
        everything = lax.all_gather(current, ("row", "col"), axis=1, tiled=True)
        x_rows = lax.dynamic_slice_in_dim(everything, row_at * row_len, row_len, 1)
        x_cols = lax.dynamic_slice_in_dim(
            everything, col_at * row_len * ratio_k, row_len * ratio_k, 1
        )
        pull_terms, stress = guttman_terms(dissim, x_rows, x_cols)
        new_share, stress_share = (
            lax.psum_scatter(pull_terms, "col", scatter_dimension=1, tiled=True),
            lax.psum_scatter(stress, "col", scatter_dimension=0, tiled=True),
        )
        current = new_share / molecules
        row_stress = stress_share / molecules
    local_stress = jnp.sum(row_stress)
    stress_total, dissim_total = lax.psum((local_stress, dissim_sq), ("row", "col"))
    stress_norm = molecules * stress_total / dissim_total
    return (current, row_stress, stress_norm)


def solution(mesh):
    return jax.shard_map(
        on_device,
        mesh=mesh,
        in_specs=(P(("row", "col"), None), P(None, ("row", "col"))),
        out_specs=(P(None, ("row", "col")), P(("row", "col")), P()),
        check_vma=False,
    )
```

profile of v0, /device:TPU:0, one launch (start us, length us, event | category | flops | bytes accessed | tf_op | source)
XLA Modules:
  0.0 698.3 jit_solution(13126097829784607838)
XLA Ops:
  7.2 0.7 all-gather.6.cloned.1.call-update
  7.9 0.7 all-gather.4.cloned.1.call-update
  8.7 84.4 %all-gather.6.cloned.1.call-done = bf16[2048,1024]{1,0:T(8,128)(2,1)} async-done(((bf16[512,1024]{1,0:T(8,128)(2,1)}), bf16[2048,1024]{1,0:T(8,128)(2,1)}) %all-gather.6.cloned.1.call-update) | async-done | bytes 4194320 | tf_op jit(solution)/shard_map/all_gather | solution.py:74
  93.1 6.0 broadcast_select_fusion.1
  99.1 3.1 fusion.13
  102.2 54.3 %all-gather.4.cloned.1.call-done = f32[64,16384]{1,0:T(8,128)} async-done(((f32[64,512]{1,0:T(8,128)}), f32[64,16384]{1,0:T(8,128)}) %all-gather.4.cloned.1.call-update) | async-done | bytes 4194320 | tf_op jit(solution)/shard_map/all_gather | solution.py:85
  156.5 1.1 constant_dynamic-slice_fusion.5
  157.5 0.4 reshape.34
  157.9 1.4 multiply_reduce_fusion.4
  159.3 126.3 %all-reduce.5.cloned.1.call-done = (bf16[2048,1024]{1,0:T(8,128)(2,1)}, bf16[2048,1024]{1,0:T(8,128)(2,1)}) async-done(((bf16[2048,1024]{1,0:T(8,128)(2,1)}, bf16[2048,1024]{1,0:T(8,128)(2,1)}), (bf16[2048,1024]{1,0:T(8,128)(2,1)}, bf16[2048,1024]{1,0:T(8,128)(2,1)})) %all-reduce.5.cloned.1.call-update) | async-done | bytes 8388624 | tf_op jit(solution)/shard_map/psum | solution.py:13
  285.5 5.3 fusion.11
  290.9 11.4 %fusion.9 = f32[2048,2048]{0,1:T(8,128)S(1)} fusion(bf16[2048,1024]{1,0:T(8,128)(2,1)} %get-tuple-element.146, bf16[2048,1024]{1,0:T(8,128)(2,1)S(1)} %copy-done, f32[2048]{0:T(1024)S(1)} %get-tuple-element.161, f32[2048]{0:T(1024)S(1)} %fusion.13), kind=kOutput, calls=%fused_computation.25 | convolution fusion | flops 8606711808 | bytes 25182208 | tf_op jit(solution)/shard_map/dot_general | solution.py:22
  302.3 14.4 %fusion.10 = f32[2048,2048]{0,1:T(8,128)} fusion(bf16[2048,1024]{1,0:T(8,128)(2,1)} %get-tuple-element.145, bf16[2048,1024]{1,0:T(8,128)(2,1)S(1)} %copy-done, f32[2048]{0:T(1024)S(1)} %get-tuple-element.160, f32[2048]{0:T(1024)S(1)} %fusion.13), kind=kOutput, calls=%fused_computation.26 | convolution fusion | flops 8606711808 | bytes 25182208 | tf_op jit(solution)/shard_map/dot_general | solution.py:22
  316.7 20.2 %multiply_reduce_fusion.2 = (f32[]{:T(128)}, f32[2048,4096]{0,1:T(8,128)}) fusion(f32[2048,2048]{0,1:T(8,128)} %fusion.10, f32[2048,2048]{0,1:T(8,128)S(1)} %fusion.9), kind=kLoop, calls=%fused_computation.22 | loop fusion | flops 25165824 | bytes 67108864 | tf_op jit(solution)/shard_map/reduce_sum | solution.py:81
  336.9 31.1 %copy.33 = f32[2048,4096]{1,0:T(8,128)} copy(f32[2048,4096]{0,1:T(8,128)} %get-tuple-element.157) | data formatting | bytes 67108864 | tf_op jit(solution)/shard_map/while | solution.py:61
  368.0 78.5 %while.22 = (s32[]{:T(128)}, f32[4,64,512]{2,1,0:T(8,128)S(1)}, f32[4,64,512]{2,0,1:T(4,128)S(1)}, f32[4,512,4096]{2,1,0:T(8,128)}, f32[4096]{0:T(1024)S(1)}, /*index=5*/f32[64,4096]{1,0:T(8,128)S(1)}, s32[]{:T(128)}) while((s32[]{:T(128)}, f32[4,64,512]{2,1,0:T(8,128)S(1)}, f32[4,64,512]{2,0,1:T(4,128)S(1)}, f32[4,512,4096]{2,1,0:T(8,128)}, ...), condition=%wide.region_6.7_spmd, body=%wide.region_3.6_spmd.sunk | while | flops 3233938432 | bytes 28074072 | solution.py:61
  368.4 11.1 %fusion.37 = (f32[512]{0:T(512)S(1)}, f32[512,4096]{1,0:T(8,128)S(1)}) fusion(f32[64,4096]{1,0:T(8,128)S(1)} %get-tuple-element.271, f32[1,64,512]{2,0,1:T(1,128)S(1)} %constant_dynamic-slice_fusion.10, f32[4096]{0:T(1024)S(1)} %get-tuple-element.270, f32[512]{0:T(512)S(1)} %multiply_reduce_fusion.7, f32[4,512,4096]{2,1,0:T(8,128)} %get-tuple-element.269, ...), kind=kOutput, calls=%fused_computation.45.clone.1 | convolution fusion | flops 1623195136 | bytes 17977348 | tf_op jit(solution)/shard_map/while/body/eval_jaxpr/dot_general | solution.py:39
  379.6 8.2 %fusion.38 = f32[4,64,512]{2,1,0:T(8,128)S(1)} fusion(f32[4,64,512]{2,1,0:T(8,128)S(1)} %get-tuple-element.260, s32[]{:T(128)} %get-tuple-element.259, f32[512,4096]{1,0:T(8,128)S(1)} %get-tuple-element.240, f32[64,4096]{1,0:T(8,128)S(1)} %get-tuple-element.271, f32[1,64,512]{2,0,1:T(1,128)S(1)} %constant_dynamic-slice_fusion.10, ...), kind=kOutput, calls=%fused_computation.4.clone.1 | convolution fusion | flops 1610678272 | bytes 9701380 | tf_op jit(solution)/shard_map/while/body/eval_jaxpr/dot_general | solution.py:50
  387.8 0.1 constant_dynamic-slice_fusion.10
  388.0 11.1 %fusion.37 = (f32[512]{0:T(512)S(1)}, f32[512,4096]{1,0:T(8,128)S(1)}) fusion(f32[64,4096]{1,0:T(8,128)S(1)} %get-tuple-element.271, f32[1,64,512]{2,0,1:T(1,128)S(1)} %constant_dynamic-slice_fusion.10, f32[4096]{0:T(1024)S(1)} %get-tuple-element.270, f32[512]{0:T(512)S(1)} %multiply_reduce_fusion.7, f32[4,512,4096]{2,1,0:T(8,128)} %get-tuple-element.269, ...), kind=kOutput, calls=%fused_computation.45.clone.1 | convolution fusion | flops 1623195136 | bytes 17977348 | tf_op jit(solution)/shard_map/while/body/eval_jaxpr/dot_general | solution.py:39
  399.1 8.2 %fusion.38 = f32[4,64,512]{2,1,0:T(8,128)S(1)} fusion(f32[4,64,512]{2,1,0:T(8,128)S(1)} %get-tuple-element.260, s32[]{:T(128)} %get-tuple-element.259, f32[512,4096]{1,0:T(8,128)S(1)} %get-tuple-element.240, f32[64,4096]{1,0:T(8,128)S(1)} %get-tuple-element.271, f32[1,64,512]{2,0,1:T(1,128)S(1)} %constant_dynamic-slice_fusion.10, ...), kind=kOutput, calls=%fused_computation.4.clone.1 | convolution fusion | flops 1610678272 | bytes 9701380 | tf_op jit(solution)/shard_map/while/body/eval_jaxpr/dot_general | solution.py:50
  407.5 11.1 %fusion.37 = (f32[512]{0:T(512)S(1)}, f32[512,4096]{1,0:T(8,128)S(1)}) fusion(f32[64,4096]{1,0:T(8,128)S(1)} %get-tuple-element.271, f32[1,64,512]{2,0,1:T(1,128)S(1)} %constant_dynamic-slice_fusion.10, f32[4096]{0:T(1024)S(1)} %get-tuple-element.270, f32[512]{0:T(512)S(1)} %multiply_reduce_fusion.7, f32[4,512,4096]{2,1,0:T(8,128)} %get-tuple-element.269, ...), kind=kOutput, calls=%fused_computation.45.clone.1 | convolution fusion | flops 1623195136 | bytes 17977348 | tf_op jit(solution)/shard_map/while/body/eval_jaxpr/dot_general | solution.py:39
  418.7 8.2 %fusion.38 = f32[4,64,512]{2,1,0:T(8,128)S(1)} fusion(f32[4,64,512]{2,1,0:T(8,128)S(1)} %get-tuple-element.260, s32[]{:T(128)} %get-tuple-element.259, f32[512,4096]{1,0:T(8,128)S(1)} %get-tuple-element.240, f32[64,4096]{1,0:T(8,128)S(1)} %get-tuple-element.271, f32[1,64,512]{2,0,1:T(1,128)S(1)} %constant_dynamic-slice_fusion.10, ...), kind=kOutput, calls=%fused_computation.4.clone.1 | convolution fusion | flops 1610678272 | bytes 9701380 | tf_op jit(solution)/shard_map/while/body/eval_jaxpr/dot_general | solution.py:50
  426.9 0.1 constant_dynamic-slice_fusion.10
  427.1 11.1 %fusion.37 = (f32[512]{0:T(512)S(1)}, f32[512,4096]{1,0:T(8,128)S(1)}) fusion(f32[64,4096]{1,0:T(8,128)S(1)} %get-tuple-element.271, f32[1,64,512]{2,0,1:T(1,128)S(1)} %constant_dynamic-slice_fusion.10, f32[4096]{0:T(1024)S(1)} %get-tuple-element.270, f32[512]{0:T(512)S(1)} %multiply_reduce_fusion.7, f32[4,512,4096]{2,1,0:T(8,128)} %get-tuple-element.269, ...), kind=kOutput, calls=%fused_computation.45.clone.1 | convolution fusion | flops 1623195136 | bytes 17977348 | tf_op jit(solution)/shard_map/while/body/eval_jaxpr/dot_general | solution.py:39
  438.3 8.2 %fusion.38 = f32[4,64,512]{2,1,0:T(8,128)S(1)} fusion(f32[4,64,512]{2,1,0:T(8,128)S(1)} %get-tuple-element.260, s32[]{:T(128)} %get-tuple-element.259, f32[512,4096]{1,0:T(8,128)S(1)} %get-tuple-element.240, f32[64,4096]{1,0:T(8,128)S(1)} %get-tuple-element.271, f32[1,64,512]{2,0,1:T(1,128)S(1)} %constant_dynamic-slice_fusion.10, ...), kind=kOutput, calls=%fused_computation.4.clone.1 | convolution fusion | flops 1610678272 | bytes 9701380 | tf_op jit(solution)/shard_map/while/body/eval_jaxpr/dot_general | solution.py:50
  446.5 0.8 copy.36
  447.4 21.9 %reduce-scatter.3.cloned.1.call-done = f32[64,512]{1,0:T(8,128)} async-done(((f32[64,2048]{1,0:T(8,128)}), f32[64,512]{1,0:T(8,128)}) %reduce-scatter.3.cloned.1.call-update) | async-done | bytes 131088 | tf_op jit(solution)/shard_map/reduce_scatter | solution.py:92
  469.3 1.6 broadcast_multiply_fusion.1
  471.0 62.4 %all-gather.8.cloned.1.call-done = f32[64,16384]{1,0:T(8,128)} async-done(((f32[64,512]{1,0:T(8,128)}), f32[64,16384]{1,0:T(8,128)}) %all-gather.8.cloned.1.call-update) | async-done | bytes 4194320 | tf_op jit(solution)/shard_map/all_gather | solution.py:85
  533.4 1.1 constant_dynamic-slice_fusion.3
  534.5 0.4 reshape.37
  534.8 1.4 multiply_reduce_fusion.3
  536.3 98.9 %while.23 = (s32[]{:T(128)}, f32[4,64,512]{2,1,0:T(8,128)S(1)}, f32[4,512]{1,0:T(4,128)S(1)}, f32[4,64,512]{2,0,1:T(4,128)S(1)}, f32[4,512,4096]{2,1,0:T(8,128)}...) while((s32[]{:T(128)}, f32[4,64,512]{2,1,0:T(8,128)S(1)}, ...), condition=%wide.region_13.14_spmd, body=%wide.region_9.13_spmd.sunk | while | flops 3242326528 | bytes 36469864 | solution.py:61
  536.7 13.9 %fusion.41 = (f32[512]{0:T(512)S(1)}, f32[512]{0:T(512)S(1)}, f32[512,4096]{1,0:T(8,128)S(1)}) fusion(f32[4,512,4096]{2,1,0:T(8,128)} %get-tuple-element.295, s32[]{:T(128)} %get-tuple-element.282, f32[64,4096]{1,0:T(8,128)S(1)} %get-tuple-element.297, f32[1,64,512]{2,0,1:T(1,128)S(1)} %constant_dynamic-slice_fusion.11, ...), kind=kOutput, calls=%fused_computation.11.clone.1 | convolution fusion | flops 1629486080 | bytes 17979396 | tf_op jit(solution)/shard_map/while/body/eval_jaxpr/dot_general | solution.py:39
  550.6 10.5 %fusion.42 = f32[4,64,512]{2,1,0:T(8,128)S(1)} fusion(f32[4,64,512]{2,1,0:T(8,128)S(1)} %get-tuple-element.283, s32[]{:T(128)} %get-tuple-element.282, f32[64,4096]{1,0:T(8,128)S(1)} %get-tuple-element.297, f32[1,64,512]{2,0,1:T(1,128)S(1)} %constant_dynamic-slice_fusion.11, f32[512]{0:T(512)S(1)} %get-tuple-element.249, ...), kind=kOutput, calls=%fused_computation.16.clone.1 | convolution fusion | flops 1612775424 | bytes 18091008 | tf_op jit(solution)/shard_map/while/body/eval_jaxpr/dot_general | solution.py:50
  561.4 13.9 %fusion.41 = (f32[512]{0:T(512)S(1)}, f32[512]{0:T(512)S(1)}, f32[512,4096]{1,0:T(8,128)S(1)}) fusion(f32[4,512,4096]{2,1,0:T(8,128)} %get-tuple-element.295, s32[]{:T(128)} %get-tuple-element.282, f32[64,4096]{1,0:T(8,128)S(1)} %get-tuple-element.297, f32[1,64,512]{2,0,1:T(1,128)S(1)} %constant_dynamic-slice_fusion.11, ...), kind=kOutput, calls=%fused_computation.11.clone.1 | convolution fusion | flops 1629486080 | bytes 17979396 | tf_op jit(solution)/shard_map/while/body/eval_jaxpr/dot_general | solution.py:39
  575.3 10.5 %fusion.42 = f32[4,64,512]{2,1,0:T(8,128)S(1)} fusion(f32[4,64,512]{2,1,0:T(8,128)S(1)} %get-tuple-element.283, s32[]{:T(128)} %get-tuple-element.282, f32[64,4096]{1,0:T(8,128)S(1)} %get-tuple-element.297, f32[1,64,512]{2,0,1:T(1,128)S(1)} %constant_dynamic-slice_fusion.11, f32[512]{0:T(512)S(1)} %get-tuple-element.249, ...), kind=kOutput, calls=%fused_computation.16.clone.1 | convolution fusion | flops 1612775424 | bytes 18091008 | tf_op jit(solution)/shard_map/while/body/eval_jaxpr/dot_general | solution.py:50
  586.0 13.9 %fusion.41 = (f32[512]{0:T(512)S(1)}, f32[512]{0:T(512)S(1)}, f32[512,4096]{1,0:T(8,128)S(1)}) fusion(f32[4,512,4096]{2,1,0:T(8,128)} %get-tuple-element.295, s32[]{:T(128)} %get-tuple-element.282, f32[64,4096]{1,0:T(8,128)S(1)} %get-tuple-element.297, f32[1,64,512]{2,0,1:T(1,128)S(1)} %constant_dynamic-slice_fusion.11, ...), kind=kOutput, calls=%fused_computation.11.clone.1 | convolution fusion | flops 1629486080 | bytes 17979396 | tf_op jit(solution)/shard_map/while/body/eval_jaxpr/dot_general | solution.py:39
  599.9 10.5 %fusion.42 = f32[4,64,512]{2,1,0:T(8,128)S(1)} fusion(f32[4,64,512]{2,1,0:T(8,128)S(1)} %get-tuple-element.283, s32[]{:T(128)} %get-tuple-element.282, f32[64,4096]{1,0:T(8,128)S(1)} %get-tuple-element.297, f32[1,64,512]{2,0,1:T(1,128)S(1)} %constant_dynamic-slice_fusion.11, f32[512]{0:T(512)S(1)} %get-tuple-element.249, ...), kind=kOutput, calls=%fused_computation.16.clone.1 | convolution fusion | flops 1612775424 | bytes 18091008 | tf_op jit(solution)/shard_map/while/body/eval_jaxpr/dot_general | solution.py:50
  610.7 13.9 %fusion.41 = (f32[512]{0:T(512)S(1)}, f32[512]{0:T(512)S(1)}, f32[512,4096]{1,0:T(8,128)S(1)}) fusion(f32[4,512,4096]{2,1,0:T(8,128)} %get-tuple-element.295, s32[]{:T(128)} %get-tuple-element.282, f32[64,4096]{1,0:T(8,128)S(1)} %get-tuple-element.297, f32[1,64,512]{2,0,1:T(1,128)S(1)} %constant_dynamic-slice_fusion.11, ...), kind=kOutput, calls=%fused_computation.11.clone.1 | convolution fusion | flops 1629486080 | bytes 17979396 | tf_op jit(solution)/shard_map/while/body/eval_jaxpr/dot_general | solution.py:39
  624.6 10.5 %fusion.42 = f32[4,64,512]{2,1,0:T(8,128)S(1)} fusion(f32[4,64,512]{2,1,0:T(8,128)S(1)} %get-tuple-element.283, s32[]{:T(128)} %get-tuple-element.282, f32[64,4096]{1,0:T(8,128)S(1)} %get-tuple-element.297, f32[1,64,512]{2,0,1:T(1,128)S(1)} %constant_dynamic-slice_fusion.11, f32[512]{0:T(512)S(1)} %get-tuple-element.249, ...), kind=kOutput, calls=%fused_computation.16.clone.1 | convolution fusion | flops 1612775424 | bytes 18091008 | tf_op jit(solution)/shard_map/while/body/eval_jaxpr/dot_general | solution.py:50
  635.2 0.8 copy.37
  636.0 0.6 dynamic-slice
  637.3 10.5 %all-reduce = f32[2048]{0:T(1024)S(1)} all-reduce(f32[2048]{0:T(1024)S(1)} %bitcast.124), channel_id=4, replica_groups=mesh['row'=8,'col'=4] {'col'}, use_global_device_ids=true, to_apply=%region_15.16.clone | all-reduce | flops 2048 | bytes 16384
  647.8 1.3 fusion.14
  649.1 38.3 %all-reduce.1 = (f32[]{:T(128)}, f32[]{:T(128)}) all-reduce(f32[]{:T(128)} %get-tuple-element.147, f32[]{:T(128)} %get-tuple-element.156), channel_id=1, replica_groups=mesh['row'=8,'col'=4] {'row','col'}, use_global_device_ids=true, to_apply=%region_17.18 | all-reduce | flops 2 | bytes 16 | tf_op jit(solution)/shard_map/psum | solution.py:98
  688.7 1.6 broadcast_multiply_fusion
  (37 shorter events, 1.6 us)
Async XLA Ops:
  7.2 85.9 %all-gather.6.cloned.1.call-start = ((), (), s32[]{:S(2)}) async-start(), calls=%async_computation.3 | async-start | bytes 5242880 | tf_op jit(solution)/shard_map/all_gather | solution.py:74
  7.9 148.6 %all-gather.4.cloned.1.call-start = ((), (), s32[]{:S(2)}) async-start(), calls=%async_computation.2 | async-start | bytes 4325376 | tf_op jit(solution)/shard_map/all_gather | solution.py:85
  8.6 276.9 %all-reduce.5.cloned.1.call-start = ((), (), s32[]{:S(2)}) async-start(), calls=%async_computation.7 | async-start | bytes 16777216 | tf_op jit(solution)/shard_map/psum | solution.py:13
  99.0 370.3 %reduce-scatter.3.cloned.1.call-start = ((), (), s32[]{:S(2)}) async-start(), calls=%async_computation.4 | async-start | bytes 655360 | tf_op jit(solution)/shard_map/reduce_scatter | solution.py:92
  285.5 5.3 copy-start
  447.4 86.0 %all-gather.8.cloned.1.call-start = ((), (), s32[]{:S(2)}) async-start(), calls=%async_computation.5 | async-start | bytes 4325376 | tf_op jit(solution)/shard_map/all_gather | solution.py:85
  470.9 217.8 %reduce-scatter.5.cloned.1.call-start = ((), (), s32[]{:S(2)}) async-start(), calls=%async_computation.6 | async-start | bytes 655360 | tf_op jit(solution)/shard_map/reduce_scatter | solution.py:92
  536.3 99.8 %copy-start.1 = (u32[32]{0:T(128)S(1)}, u32[32]{0:T(128)}, u32[]{:S(2)}) copy-start(u32[32]{0:T(128)} %constant.75) | copy-start | bytes 388
Sparse Core Ops, SparseCore 0:
  9.6 83.4 all-gather.5
  96.1 60.2 all-gather.3
  160.2 125.3 all-reduce.4
  447.5 21.7 reduce-scatter.2
  473.3 60.0 all-gather.7
  636.2 19.9 reduce-scatter.4
where the time goes:
time: 699 us; the launch traced here: 698 us
  waiting for transfers between devices  351 us (50%)
  matrix products  201 us (29%)
  blocking collectives  48.8 us (7%)
  other arithmetic  41.9 us (6%)
  local copies, waits for them, and re-layouts  37.5 us (5%)
  between operations  17.4 us (2%)
    psum x1, waiting for transfers between devices, from_root(): return lax.psum(block, axis)  126 us
    all_gather x2, waiting for transfers between devices, on_device(): everything = lax.all_gather(current, ('row', 'col'), axis=1, tiled=True)  117 us
    dot_general x8, matrix products, one_block(): lax.dot_general(x_blk, x_cols, (((0,), (0,)), ((), ())), precision=EXACT,...  100 us
    all_gather x1, waiting for transfers between devices, on_device(): feature_rows = lax.all_gather(features, 'col', axis=0, tiled=True)  84.4 us
    dot_general x8, matrix products, one_block(): lax.dot_general(x_cols, ratios, (((1,), (1,)), ((), ())), precision=EXACT...  74.9 us
    psum x1, blocking collectives, on_device(): lax.psum((local_stress, dissim_sq), ('row', 'col'))  38.3 us
    while x1, local copies, waits for them, and re-layouts, guttman_terms(): pull_terms, stress = lax.map(one_block, (dis_blocks, x_blocks))  31.1 us
    dot_general x2, matrix products, tanimoto(): lax.dot_general(left_rows, right_rows, (((1,), (1,)), ((), ())), preferre...  25.8 us
  transfers between devices with their start and end apart: 6, of which 5 were waited for; matrix products, arithmetic and copies ran while one was open for 2% of the time, Pallas kernels for 0%

commit v1 on v0

--- a/solution.py
+++ b/solution.py
@@ -71,7 +71,14 @@
     share_len = coords.shape[1]
     row_len = share_len * cols_n
     molecules = row_len * rows_n
-    feature_rows = lax.all_gather(features, "col", axis=0, tiled=True)
+    size = lax.axis_size("col")
+    route = [(i, (i + 1) % size) for i in range(size)]
+    terms = [features]
+    for far in range(1, size):
+        terms = [lax.ppermute(terms[0], "col", route), *terms]
+    result = jnp.concatenate(terms, axis=0)
+    shift = (lax.axis_index("col") + 1) * terms[-1].shape[0]
+    feature_rows = jnp.roll(result, shift, axis=0)
     rows_sq = squares_of(feature_rows)
     pieces = []
     for offset in range(ratio_k):

time: 699 us -> 652 us (0.933)
  waiting for transfers between devices: 351 us -> 285 us
  local copies, waits for them, and re-layouts: 37.5 us -> 44.9 us
    all_gather x1 -> x0, waiting for transfers between devices: 84.4 us -> none  [on_device(): feature_rows = lax.all_gather(features, 'col', axis=0, tiled=True)]
    ppermute x0 -> x3, waiting for transfers between devices: none -> 76.9 us  [on_device(): terms = [lax.ppermute(terms[0], 'col', route), *terms]]
    all_gather x2, waiting for transfers between devices: 117 us -> 60.2 us  [on_device(): everything = lax.all_gather(current, ('row', 'col'), axis=1, tiled=True)]
    unnamed x6 -> x19, local copies, waits for them, and re-layouts: 0.6 us -> 7.99 us
  transfers between devices with their start and end apart: 6 -> 8, of which waited for: 5 -> 6; matrix products, arithmetic and copies ran while one was open for 2% -> 14% of each run, Pallas kernels for 0% -> 0%
where the time goes in v1:
time: 652 us; the launch traced here: 646 us
  waiting for transfers between devices  285 us (44%)
  matrix products  204 us (31%)
  blocking collectives  48.9 us (8%)
  local copies, waits for them, and re-layouts  44.9 us (7%)
  other arithmetic  41.1 us (6%)
  between operations  18.8 us (3%)
    psum x1, waiting for transfers between devices, from_root(): return lax.psum(block, axis)  126 us
    dot_general x8, matrix products, one_block(): lax.dot_general(x_blk, x_cols, (((0,), (0,)), ((), ())), precision=EXACT,...  100 us
    ppermute x3, waiting for transfers between devices, on_device(): terms = [lax.ppermute(terms[0], 'col', route), *terms]  76.9 us
    dot_general x8, matrix products, one_block(): lax.dot_general(x_cols, ratios, (((1,), (1,)), ((), ())), precision=EXACT...  74.9 us
    all_gather x2, waiting for transfers between devices, on_device(): everything = lax.all_gather(current, ('row', 'col'), axis=1, tiled=True)  60.2 us
    psum x1, blocking collectives, on_device(): lax.psum((local_stress, dissim_sq), ('row', 'col'))  38 us
    while x1, local copies, waits for them, and re-layouts, guttman_terms(): pull_terms, stress = lax.map(one_block, (dis_blocks, x_blocks))  31.1 us
    dot_general x2, matrix products, tanimoto(): lax.dot_general(left_rows, right_rows, (((1,), (1,)), ((), ())), preferre...  28.3 us
  transfers between devices with their start and end apart: 8, of which 6 were waited for; matrix products, arithmetic and copies ran while one was open for 14% of the time, Pallas kernels for 0%

profile of v1, /device:TPU:0, one launch (start us, length us, event | category | flops | bytes accessed | tf_op | source)
XLA Modules:
  0.0 646.5 jit_solution(11102121443519563279)
XLA Ops:
  8.1 3.1 collective-permute-start
  11.1 25.4 %collective-permute-done = bf16[512,1024]{1,0:T(8,128)(2,1)S(1)} collective-permute-done((bf16[512,1024]{1,0:T(8,128)(2,1)}, bf16[512,1024]{1,0:T(8,128)(2,1)S(1)}, u32[]{:S(2)}, u32[]{:S(2)}) %collective-permute-start) | collective-permute-done | bytes 1048608 | tf_op jit(solution)/shard_map/ppermute | solution.py:78
  36.5 26.1 %collective-permute-done.1 = bf16[512,1024]{1,0:T(8,128)(2,1)S(1)} collective-permute-done((bf16[512,1024]{1,0:T(8,128)(2,1)S(1)}, bf16[512,1024]{1,0:T(8,128)(2,1)S(1)}, u32[]{:S(2)}, u32[]{:S(2)}) %collective-permute-start.1) | collective-permute-done | bytes 1048608 | tf_op jit(solution)/shard_map/ppermute | solution.py:78
  62.7 25.3 %collective-permute-done.2 = bf16[512,1024]{1,0:T(8,128)(2,1)} collective-permute-done((bf16[512,1024]{1,0:T(8,128)(2,1)S(1)}, bf16[512,1024]{1,0:T(8,128)(2,1)}, u32[]{:S(2)}, u32[]{:S(2)}) %collective-permute-start.2) | collective-permute-done | bytes 1048608 | tf_op jit(solution)/shard_map/ppermute | solution.py:78
  88.0 1.3 constant_dynamic-update-slice_fusion.7
  89.5 1.3 constant_dynamic-update-slice_fusion.4
  90.8 1.3 constant_dynamic-update-slice_fusion.3
  92.3 3.2 copy-done
  95.5 5.0 broadcast_select_fusion.1
  101.2 3.1 fusion.13
  104.3 125.7 %all-reduce.5.cloned.1.call-done = (bf16[2048,1024]{1,0:T(8,128)(2,1)}, bf16[2048,1024]{1,0:T(8,128)(2,1)}) async-done(((bf16[2048,1024]{1,0:T(8,128)(2,1)}, bf16[2048,1024]{1,0:T(8,128)(2,1)}), (bf16[2048,1024]{1,0:T(8,128)(2,1)}, bf16[2048,1024]{1,0:T(8,128)(2,1)})) %all-reduce.5.cloned.1.call-update) | async-done | bytes 8388624 | tf_op jit(solution)/shard_map/psum | solution.py:13
  230.0 5.3 fusion.11
  235.4 13.9 %fusion.9 = f32[2048,2048]{0,1:T(8,128)S(1)} fusion(f32[2048]{0:T(1024)S(1)} %get-tuple-element.161, f32[2048]{0:T(1024)S(1)} %fusion.13, bf16[2048,1024]{1,0:T(8,128)(2,1)} %get-tuple-element.146, bf16[4096,1024]{1,0:T(8,128)(2,1)} %copy-done, s32[]{:T(128)S(6)} %select_n.37), kind=kOutput, calls=%fused_computation.25 | convolution fusion | flops 8606711808 | bytes 25182212 | tf_op jit(solution)/shard_map/dot_general | solution.py:22
  249.3 14.4 %fusion.10 = f32[2048,2048]{0,1:T(8,128)} fusion(f32[2048]{0:T(1024)S(1)} %get-tuple-element.160, f32[2048]{0:T(1024)S(1)} %fusion.13, bf16[2048,1024]{1,0:T(8,128)(2,1)} %get-tuple-element.145, bf16[4096,1024]{1,0:T(8,128)(2,1)S(1)} %bitcast.112, s32[]{:T(128)S(6)} %select_n.37), kind=kOutput, calls=%fused_computation.26 | convolution fusion | flops 8606711808 | bytes 25182212 | tf_op jit(solution)/shard_map/dot_general | solution.py:22
  263.7 20.3 %multiply_reduce_fusion.2 = (f32[]{:T(128)}, f32[2048,4096]{0,1:T(8,128)}) fusion(f32[2048,2048]{0,1:T(8,128)} %fusion.10, f32[2048,2048]{0,1:T(8,128)S(1)} %fusion.9), kind=kLoop, calls=%fused_computation.22 | loop fusion | flops 25165824 | bytes 67108864 | tf_op jit(solution)/shard_map/reduce_sum | solution.py:88
  284.0 31.1 %copy.33 = f32[2048,4096]{1,0:T(8,128)} copy(f32[2048,4096]{0,1:T(8,128)} %get-tuple-element.157) | data formatting | bytes 67108864 | tf_op jit(solution)/shard_map/while | solution.py:61
  315.1 1.1 constant_dynamic-slice_fusion.5
  316.6 1.4 multiply_reduce_fusion.4
  318.0 78.4 %while.22 = (s32[]{:T(128)}, f32[4,64,512]{2,1,0:T(8,128)S(1)}, f32[4,64,512]{2,0,1:T(4,128)S(1)}, f32[4,512,4096]{2,1,0:T(8,128)}, f32[4096]{0:T(1024)S(1)}, /*index=5*/f32[64,4096]{1,0:T(8,128)S(1)}, s32[]{:T(128)}) while((s32[]{:T(128)}, f32[4,64,512]{2,1,0:T(8,128)S(1)}, f32[4,64,512]{2,0,1:T(4,128)S(1)}, f32[4,512,4096]{2,1,0:T(8,128)}, ...), condition=%wide.region_6.7_spmd, body=%wide.region_3.6_spmd.sunk | while | flops 3233938432 | bytes 28074072 | solution.py:61
  318.3 11.2 %fusion.39 = (f32[512]{0:T(512)S(1)}, f32[512,4096]{1,0:T(8,128)S(1)}) fusion(f32[64,4096]{1,0:T(8,128)S(1)} %get-tuple-element.271, f32[1,64,512]{2,0,1:T(1,128)S(1)} %constant_dynamic-slice_fusion.10, f32[4096]{0:T(1024)S(1)} %get-tuple-element.270, f32[512]{0:T(512)S(1)} %multiply_reduce_fusion.7, f32[4,512,4096]{2,1,0:T(8,128)} %get-tuple-element.269, ...), kind=kOutput, calls=%fused_computation.57.clone.1 | convolution fusion | flops 1623195136 | bytes 17977348 | tf_op jit(solution)/shard_map/while/body/eval_jaxpr/dot_general | solution.py:39
  329.5 8.2 %fusion.40 = f32[4,64,512]{2,1,0:T(8,128)S(1)} fusion(f32[4,64,512]{2,1,0:T(8,128)S(1)} %get-tuple-element.260, s32[]{:T(128)} %get-tuple-element.259, f32[512,4096]{1,0:T(8,128)S(1)} %get-tuple-element.240, f32[64,4096]{1,0:T(8,128)S(1)} %get-tuple-element.271, f32[1,64,512]{2,0,1:T(1,128)S(1)} %constant_dynamic-slice_fusion.10, ...), kind=kOutput, calls=%fused_computation.4.clone.1 | convolution fusion | flops 1610678272 | bytes 9701380 | tf_op jit(solution)/shard_map/while/body/eval_jaxpr/dot_general | solution.py:50
  337.9 11.1 %fusion.39 = (f32[512]{0:T(512)S(1)}, f32[512,4096]{1,0:T(8,128)S(1)}) fusion(f32[64,4096]{1,0:T(8,128)S(1)} %get-tuple-element.271, f32[1,64,512]{2,0,1:T(1,128)S(1)} %constant_dynamic-slice_fusion.10, f32[4096]{0:T(1024)S(1)} %get-tuple-element.270, f32[512]{0:T(512)S(1)} %multiply_reduce_fusion.7, f32[4,512,4096]{2,1,0:T(8,128)} %get-tuple-element.269, ...), kind=kOutput, calls=%fused_computation.57.clone.1 | convolution fusion | flops 1623195136 | bytes 17977348 | tf_op jit(solution)/shard_map/while/body/eval_jaxpr/dot_general | solution.py:39
  349.0 8.2 %fusion.40 = f32[4,64,512]{2,1,0:T(8,128)S(1)} fusion(f32[4,64,512]{2,1,0:T(8,128)S(1)} %get-tuple-element.260, s32[]{:T(128)} %get-tuple-element.259, f32[512,4096]{1,0:T(8,128)S(1)} %get-tuple-element.240, f32[64,4096]{1,0:T(8,128)S(1)} %get-tuple-element.271, f32[1,64,512]{2,0,1:T(1,128)S(1)} %constant_dynamic-slice_fusion.10, ...), kind=kOutput, calls=%fused_computation.4.clone.1 | convolution fusion | flops 1610678272 | bytes 9701380 | tf_op jit(solution)/shard_map/while/body/eval_jaxpr/dot_general | solution.py:50
  357.4 11.1 %fusion.39 = (f32[512]{0:T(512)S(1)}, f32[512,4096]{1,0:T(8,128)S(1)}) fusion(f32[64,4096]{1,0:T(8,128)S(1)} %get-tuple-element.271, f32[1,64,512]{2,0,1:T(1,128)S(1)} %constant_dynamic-slice_fusion.10, f32[4096]{0:T(1024)S(1)} %get-tuple-element.270, f32[512]{0:T(512)S(1)} %multiply_reduce_fusion.7, f32[4,512,4096]{2,1,0:T(8,128)} %get-tuple-element.269, ...), kind=kOutput, calls=%fused_computation.57.clone.1 | convolution fusion | flops 1623195136 | bytes 17977348 | tf_op jit(solution)/shard_map/while/body/eval_jaxpr/dot_general | solution.py:39
  368.6 8.2 %fusion.40 = f32[4,64,512]{2,1,0:T(8,128)S(1)} fusion(f32[4,64,512]{2,1,0:T(8,128)S(1)} %get-tuple-element.260, s32[]{:T(128)} %get-tuple-element.259, f32[512,4096]{1,0:T(8,128)S(1)} %get-tuple-element.240, f32[64,4096]{1,0:T(8,128)S(1)} %get-tuple-element.271, f32[1,64,512]{2,0,1:T(1,128)S(1)} %constant_dynamic-slice_fusion.10, ...), kind=kOutput, calls=%fused_computation.4.clone.1 | convolution fusion | flops 1610678272 | bytes 9701380 | tf_op jit(solution)/shard_map/while/body/eval_jaxpr/dot_general | solution.py:50
  377.0 11.1 %fusion.39 = (f32[512]{0:T(512)S(1)}, f32[512,4096]{1,0:T(8,128)S(1)}) fusion(f32[64,4096]{1,0:T(8,128)S(1)} %get-tuple-element.271, f32[1,64,512]{2,0,1:T(1,128)S(1)} %constant_dynamic-slice_fusion.10, f32[4096]{0:T(1024)S(1)} %get-tuple-element.270, f32[512]{0:T(512)S(1)} %multiply_reduce_fusion.7, f32[4,512,4096]{2,1,0:T(8,128)} %get-tuple-element.269, ...), kind=kOutput, calls=%fused_computation.57.clone.1 | convolution fusion | flops 1623195136 | bytes 17977348 | tf_op jit(solution)/shard_map/while/body/eval_jaxpr/dot_general | solution.py:39
  388.2 8.2 %fusion.40 = f32[4,64,512]{2,1,0:T(8,128)S(1)} fusion(f32[4,64,512]{2,1,0:T(8,128)S(1)} %get-tuple-element.260, s32[]{:T(128)} %get-tuple-element.259, f32[512,4096]{1,0:T(8,128)S(1)} %get-tuple-element.240, f32[64,4096]{1,0:T(8,128)S(1)} %get-tuple-element.271, f32[1,64,512]{2,0,1:T(1,128)S(1)} %constant_dynamic-slice_fusion.10, ...), kind=kOutput, calls=%fused_computation.4.clone.1 | convolution fusion | flops 1610678272 | bytes 9701380 | tf_op jit(solution)/shard_map/while/body/eval_jaxpr/dot_general | solution.py:50
  396.4 0.8 copy.36
  397.3 21.9 %reduce-scatter.3.cloned.1.call-done = f32[64,512]{1,0:T(8,128)} async-done(((f32[64,2048]{1,0:T(8,128)}), f32[64,512]{1,0:T(8,128)}) %reduce-scatter.3.cloned.1.call-update) | async-done | bytes 131088 | tf_op jit(solution)/shard_map/reduce_scatter | solution.py:99
  419.2 1.6 broadcast_multiply_fusion.1
  420.9 60.2 %all-gather.5.cloned.1.call-done = f32[64,16384]{1,0:T(8,128)} async-done(((f32[64,512]{1,0:T(8,128)}), f32[64,16384]{1,0:T(8,128)}) %all-gather.5.cloned.1.call-update) | async-done | bytes 4194320 | tf_op jit(solution)/shard_map/all_gather | solution.py:92
  481.1 1.1 constant_dynamic-slice_fusion.3
  482.5 1.4 multiply_reduce_fusion.3
  484.0 98.8 %while.23 = (s32[]{:T(128)}, f32[4,64,512]{2,1,0:T(8,128)S(1)}, f32[4,512]{1,0:T(4,128)S(1)}, f32[4,64,512]{2,0,1:T(4,128)S(1)}, f32[4,512,4096]{2,1,0:T(8,128)}...) while((s32[]{:T(128)}, f32[4,64,512]{2,1,0:T(8,128)S(1)}, ...), condition=%wide.region_13.14_spmd, body=%wide.region_9.13_spmd.sunk | while | flops 3242326528 | bytes 36469864 | solution.py:61
  484.4 13.9 %fusion.43 = (f32[512]{0:T(512)S(1)}, f32[512]{0:T(512)S(1)}, f32[512,4096]{1,0:T(8,128)S(1)}) fusion(f32[4,512,4096]{2,1,0:T(8,128)} %get-tuple-element.295, s32[]{:T(128)} %get-tuple-element.282, f32[64,4096]{1,0:T(8,128)S(1)} %get-tuple-element.297, f32[1,64,512]{2,0,1:T(1,128)S(1)} %constant_dynamic-slice_fusion.11, ...), kind=kOutput, calls=%fused_computation.11.clone.1 | convolution fusion | flops 1629486080 | bytes 17979396 | tf_op jit(solution)/shard_map/while/body/eval_jaxpr/dot_general | solution.py:39
  498.3 10.5 %fusion.44 = f32[4,64,512]{2,1,0:T(8,128)S(1)} fusion(f32[4,64,512]{2,1,0:T(8,128)S(1)} %get-tuple-element.283, s32[]{:T(128)} %get-tuple-element.282, f32[64,4096]{1,0:T(8,128)S(1)} %get-tuple-element.297, f32[1,64,512]{2,0,1:T(1,128)S(1)} %constant_dynamic-slice_fusion.11, f32[512]{0:T(512)S(1)} %get-tuple-element.249, ...), kind=kOutput, calls=%fused_computation.16.clone.1 | convolution fusion | flops 1612775424 | bytes 18091008 | tf_op jit(solution)/shard_map/while/body/eval_jaxpr/dot_general | solution.py:50
  509.0 13.9 %fusion.43 = (f32[512]{0:T(512)S(1)}, f32[512]{0:T(512)S(1)}, f32[512,4096]{1,0:T(8,128)S(1)}) fusion(f32[4,512,4096]{2,1,0:T(8,128)} %get-tuple-element.295, s32[]{:T(128)} %get-tuple-element.282, f32[64,4096]{1,0:T(8,128)S(1)} %get-tuple-element.297, f32[1,64,512]{2,0,1:T(1,128)S(1)} %constant_dynamic-slice_fusion.11, ...), kind=kOutput, calls=%fused_computation.11.clone.1 | convolution fusion | flops 1629486080 | bytes 17979396 | tf_op jit(solution)/shard_map/while/body/eval_jaxpr/dot_general | solution.py:39
  522.9 10.5 %fusion.44 = f32[4,64,512]{2,1,0:T(8,128)S(1)} fusion(f32[4,64,512]{2,1,0:T(8,128)S(1)} %get-tuple-element.283, s32[]{:T(128)} %get-tuple-element.282, f32[64,4096]{1,0:T(8,128)S(1)} %get-tuple-element.297, f32[1,64,512]{2,0,1:T(1,128)S(1)} %constant_dynamic-slice_fusion.11, f32[512]{0:T(512)S(1)} %get-tuple-element.249, ...), kind=kOutput, calls=%fused_computation.16.clone.1 | convolution fusion | flops 1612775424 | bytes 18091008 | tf_op jit(solution)/shard_map/while/body/eval_jaxpr/dot_general | solution.py:50
  533.7 13.9 %fusion.43 = (f32[512]{0:T(512)S(1)}, f32[512]{0:T(512)S(1)}, f32[512,4096]{1,0:T(8,128)S(1)}) fusion(f32[4,512,4096]{2,1,0:T(8,128)} %get-tuple-element.295, s32[]{:T(128)} %get-tuple-element.282, f32[64,4096]{1,0:T(8,128)S(1)} %get-tuple-element.297, f32[1,64,512]{2,0,1:T(1,128)S(1)} %constant_dynamic-slice_fusion.11, ...), kind=kOutput, calls=%fused_computation.11.clone.1 | convolution fusion | flops 1629486080 | bytes 17979396 | tf_op jit(solution)/shard_map/while/body/eval_jaxpr/dot_general | solution.py:39
  547.6 10.5 %fusion.44 = f32[4,64,512]{2,1,0:T(8,128)S(1)} fusion(f32[4,64,512]{2,1,0:T(8,128)S(1)} %get-tuple-element.283, s32[]{:T(128)} %get-tuple-element.282, f32[64,4096]{1,0:T(8,128)S(1)} %get-tuple-element.297, f32[1,64,512]{2,0,1:T(1,128)S(1)} %constant_dynamic-slice_fusion.11, f32[512]{0:T(512)S(1)} %get-tuple-element.249, ...), kind=kOutput, calls=%fused_computation.16.clone.1 | convolution fusion | flops 1612775424 | bytes 18091008 | tf_op jit(solution)/shard_map/while/body/eval_jaxpr/dot_general | solution.py:50
  558.3 13.9 %fusion.43 = (f32[512]{0:T(512)S(1)}, f32[512]{0:T(512)S(1)}, f32[512,4096]{1,0:T(8,128)S(1)}) fusion(f32[4,512,4096]{2,1,0:T(8,128)} %get-tuple-element.295, s32[]{:T(128)} %get-tuple-element.282, f32[64,4096]{1,0:T(8,128)S(1)} %get-tuple-element.297, f32[1,64,512]{2,0,1:T(1,128)S(1)} %constant_dynamic-slice_fusion.11, ...), kind=kOutput, calls=%fused_computation.11.clone.1 | convolution fusion | flops 1629486080 | bytes 17979396 | tf_op jit(solution)/shard_map/while/body/eval_jaxpr/dot_general | solution.py:39
  572.3 10.5 %fusion.44 = f32[4,64,512]{2,1,0:T(8,128)S(1)} fusion(f32[4,64,512]{2,1,0:T(8,128)S(1)} %get-tuple-element.283, s32[]{:T(128)} %get-tuple-element.282, f32[64,4096]{1,0:T(8,128)S(1)} %get-tuple-element.297, f32[1,64,512]{2,0,1:T(1,128)S(1)} %constant_dynamic-slice_fusion.11, f32[512]{0:T(512)S(1)} %get-tuple-element.249, ...), kind=kOutput, calls=%fused_computation.16.clone.1 | convolution fusion | flops 1612775424 | bytes 18091008 | tf_op jit(solution)/shard_map/while/body/eval_jaxpr/dot_general | solution.py:50
  582.8 0.8 copy.37
  583.7 0.6 dynamic-slice
  584.9 10.9 %all-reduce = f32[2048]{0:T(1024)S(1)} all-reduce(f32[2048]{0:T(1024)S(1)} %bitcast.120), channel_id=4, replica_groups=mesh['row'=8,'col'=4] {'col'}, use_global_device_ids=true, to_apply=%region_15.16.clone | all-reduce | flops 2048 | bytes 16384
  595.8 1.3 fusion.18
  597.1 38.0 %all-reduce.1 = (f32[]{:T(128)}, f32[]{:T(128)}) all-reduce(f32[]{:T(128)} %get-tuple-element.147, f32[]{:T(128)} %get-tuple-element.156), channel_id=1, replica_groups=mesh['row'=8,'col'=4] {'row','col'}, use_global_device_ids=true, to_apply=%region_17.18 | all-reduce | flops 2 | bytes 16 | tf_op jit(solution)/shard_map/psum | solution.py:105
  636.4 1.6 broadcast_multiply_fusion
  (55 shorter events, 3.4 us)
Async XLA Ops:
  8.0 84.2 %copy-start.1 = (bf16[512,1024]{1,0:T(8,128)(2,1)S(1)}, bf16[512,1024]{1,0:T(8,128)(2,1)}, u32[]{:S(2)}) copy-start(bf16[512,1024]{1,0:T(8,128)(2,1)} %param.6) | copy-start | bytes 3145732
  8.0 222.0 %all-reduce.5.cloned.1.call-start = ((), (), s32[]{:S(2)}) async-start(), calls=%async_computation.6 | async-start | bytes 16777216 | tf_op jit(solution)/shard_map/psum | solution.py:13
  8.1 28.5 %collective-permute-start = (bf16[512,1024]{1,0:T(8,128)(2,1)}, bf16[512,1024]{1,0:T(8,128)(2,1)S(1)}, u32[]{:S(2)}, u32[]{:S(2)}) collective-permute-start(bf16[512,1024]{1,0:T(8,128)(2,1)} %param.6), channel_id=1, source_target_pairs={{0,1},{1,2},{2,3},{3,0},{4,5},{5,6},{6,7},{7,4},{8,9},{9,10},{10,1... | collective-permute-start | bytes 3145736 | tf_op jit(solution)/shard_map/ppermute | solution.py:78
  36.5 26.1 %collective-permute-start.1 = (bf16[512,1024]{1,0:T(8,128)(2,1)S(1)}, bf16[512,1024]{1,0:T(8,128)(2,1)S(1)}, u32[]{:S(2)}, u32[]{:S(2)}) collective-permute-start(bf16[512,1024]{1,0:T(8,128)(2,1)S(1)} %collective-permute-done), channel_id=1, source_target_pairs={{0,1},{1,2},{2,3},{3,0},{4,5},{5,6},{6,7},{7,4},{8,9},{9,10},{10,1... | collective-permute-start | bytes 3145736 | tf_op jit(solution)/shard_map/ppermute | solution.py:78
  62.7 25.3 %collective-permute-start.2 = (bf16[512,1024]{1,0:T(8,128)(2,1)S(1)}, bf16[512,1024]{1,0:T(8,128)(2,1)}, u32[]{:S(2)}, u32[]{:S(2)}) collective-permute-start(bf16[512,1024]{1,0:T(8,128)(2,1)S(1)} %collective-permute-done.1), channel_id=1, source_target_pairs={{0,1},{1,2},{2,3},{3,0},{4,5},{5,6},{6,7},{7,4},{8,9},{9,10},{10,1... | collective-permute-start | bytes 3145736 | tf_op jit(solution)/shard_map/ppermute | solution.py:78
  92.3 3.2 copy-start
  100.6 214.5 %all-gather.3.cloned.1.call-start = ((), (), s32[]{:S(2)}) async-start(), calls=%async_computation.2 | async-start | bytes 4325376 | tf_op jit(solution)/shard_map/all_gather | solution.py:92
  101.2 318.1 %reduce-scatter.3.cloned.1.call-start = ((), (), s32[]{:S(2)}) async-start(), calls=%async_computation.3 | async-start | bytes 655360 | tf_op jit(solution)/shard_map/reduce_scatter | solution.py:99
  230.0 19.3 %slice-start = ((s8[8388608]{0:T(1024)(128)(4,1)}), s8[4194304]{0:T(1024)(128)(4,1)S(1)}, s32[]{:S(2)}) async-start(s8[8388608]{0:T(1024)(128)(4,1)} %bitcast.111), calls=%async_computation.7 | async-start | bytes 8388608
  235.4 14.0 %slice-start.1 = ((s8[8388608]{0:T(1024)(128)(4,1)}), s8[4194304]{0:T(1024)(128)(4,1)S(1)}, s32[]{:S(2)}) async-start(s8[8388608]{0:T(1024)(128)(4,1)} %bitcast.111), calls=%async_computation.8 | async-start | bytes 8388608
  397.3 83.8 %all-gather.5.cloned.1.call-start = ((), (), s32[]{:S(2)}) async-start(), calls=%async_computation.4 | async-start | bytes 4325376 | tf_op jit(solution)/shard_map/all_gather | solution.py:92
  420.8 215.6 %reduce-scatter.5.cloned.1.call-start = ((), (), s32[]{:S(2)}) async-start(), calls=%async_computation.5 | async-start | bytes 655360 | tf_op jit(solution)/shard_map/reduce_scatter | solution.py:99
  484.0 99.7 %copy-start.2 = (u32[32]{0:T(128)S(1)}, u32[32]{0:T(128)}, u32[]{:S(2)}) copy-start(u32[32]{0:T(128)} %constant.97) | copy-start | bytes 388
Sparse Core Ops, SparseCore 0:
  100.7 129.2 all-reduce.4
  397.4 21.7 reduce-scatter.2
  583.8 20.1 reduce-scatter.4
Sparse Core Ops, SparseCore 1:
  104.6 76.0 all-gather.2
  420.9 60.1 all-gather.4
